TPU v7x, 512 devices: a whole 4x4x16 slice. The times are simulated.
512 devices in a mesh: lon: 32 (over y, x, core), lat: 8 (over z_lo), depth: 2 (over z_hi).
Axes of the slice: x: 4, y: 4, z: 16 (z_hi: 2, z_lo: 8; z = z_hi * 8 + z_lo), core: 2. Of those that a mesh axis runs over, the one named last changes fastest.
Arguments:
- adj_temp: float32 [96, 64, 4096], P('depth', 'lat', 'lon'), may hold values from -6 to 6
- adj_salt: float32 [96, 64, 4096], P('depth', 'lat', 'lon'), may hold values from -6 to 6
- adj_zonal: float32 [96, 64, 4096], P('depth', 'lat', 'lon'), may hold values from -6 to 6
- adj_merid: float32 [96, 64, 4096], P('depth', 'lat', 'lon'), may hold values from -6 to 6
- east_speed: float32 [96, 64, 4096], P('depth', 'lat', 'lon'), may hold values from -4 to 4
- north_speed: float32 [96, 64, 4096], P('depth', 'lat', 'lon'), may hold values from -4 to 4
- branch_flags: int32 [2, 96, 64, 4096], P(None, 'depth', 'lat', 'lon'), may hold values from 0 to 8
- sea_mask: int32 [96, 64, 4096], P('depth', 'lat', 'lon'), may hold values 0 or 1
- block_inverse: float32 [64, 96, 48], P('lat', 'depth'), may hold values from -1 to 1, as said below
- coupling: float32 [64], P('lat'), may hold values from 0.3 to 0.9
Outputs:
- grad_temp: float32 [96, 64, 4096], P('depth', 'lat', 'lon')
- grad_salt: float32 [96, 64, 4096], P('depth', 'lat', 'lon')
- grad_zonal: float32 [96, 64, 4096], P('depth', 'lat', 'lon')
- grad_merid: float32 [96, 64, 4096], P('depth', 'lat', 'lon')
Inputs may be any that keep to these rules, and one draw needn't show every extreme that they name: `branch_flags`: a flag is 3 times the branch of the north face plus the branch of the east face. `sea_mask`: 1 marks a sea cell. `block_inverse`: the diagonal entries of every 48 x 48 block lie between 0.4 and 1, the other entries between -0.5 / 48 and 0.5 / 48.
All inputs are finite; a program needn't handle non-finite values. No bound on the sum of `sea_mask` on one device may be relied on, other than what follows from the above.
Results may differ from a plain program's by a relative error of at most 0.00016.
Values sent between devices are 32-bit elements; how exact they have to be, the bound alone decides.
A program may use at most 64 MiB of HBM per device.

v0:
```python
import jax
import jax.numpy as jnp
from jax import lax
from jax.sharding import PartitionSpec as P

STEPS = 2


advect_scale = 0.25
diffusion = 0.5
gravity = 0.1
pressure_scale = 1.0
viscosity = 0.1
haline = 0.8


def partner(value, axis, apart):
    mask = 2**apart
    pairs = [(source, source ^ mask) for source in range(lax.axis_size(axis))]
    return lax.ppermute(value, axis, pairs)


def with_halo(block, sides, width, periodic):
    for axis, dim in sides:
        count = lax.axis_size(axis)
        forward = [(i, i + 1) for i in range(count - 1)]
        if periodic:
            forward.append((count - 1, 0))
        backward = [(target, source) for source, target in forward]
        low = lax.ppermute(
            lax.slice_in_dim(block, block.shape[dim] - width, None, axis=dim), axis, forward
        )
        high = lax.ppermute(lax.slice_in_dim(block, 0, width, axis=dim), axis, backward)
        block = jnp.concatenate([low, block, high], axis=dim)
    return block


def entering(part, axis, combine, identity):
    count = lax.axis_size(axis)
    place = lax.axis_index(axis)
    ahead = count - 1 - place
    gathered = lax.all_gather(part, axis)
    state = jnp.zeros_like(part) + jnp.asarray(identity, part.dtype)

    def one(hop, state):
        source = count - 1 - hop
        return combine(state, lax.dynamic_index_in_dim(gathered, source, 0, False))

    return lax.fori_loop(0, ahead, one, state)


def project(stack, inverse):
    return jnp.einsum("yjk,fjyx->fkyx", inverse, stack, precision=lax.Precision.HIGHEST)


def interface(projected, inverse, edge):
    spike_row = lax.dynamic_index_in_dim(inverse, edge, 1, keepdims=False)
    corner = lax.dynamic_index_in_dim(spike_row, edge, 1, keepdims=False)
    plane = lax.dynamic_index_in_dim(projected, edge, 1, keepdims=False)
    return (spike_row, corner, plane)


def finish(projected, spike_row, corner, plane, other_corner, other_plane, coupling):
    divisor = 1.0 - coupling * coupling * corner * other_corner
    carried = (other_plane + (coupling * other_corner)[:, None] * plane) / divisor[:, None]
    return projected + (coupling[:, None] * spike_row).T[None, :, :, None] * carried[:, None]


def face_terms(lon_extra, lat_extra, east_self, north_self, sea):
    sea_lon = lon_extra[0]
    sea_lat = lat_extra[0]
    east_own = east_self * sea_lon[..., 2:][None]
    west_own = lon_extra[1:, ..., :-2] * sea[None]
    north_own = north_self * sea_lat[:, 2:, :][None]
    south_own = lat_extra[1:, :, :-2, :] * sea[None]
    return (east_own, west_own, north_own, south_own, sea_lon, sea_lat)


def add_sums(earlier, later):
    return earlier + later


def on_device(
    adj_temp,
    adj_salt,
    adj_zonal,
    adj_merid,
    east_speed,
    north_speed,
    branch_flags,
    sea_mask,
    block_inverse,
    coupling,
):
    levels, rows, cols = adj_temp.shape
    sea = sea_mask.astype(jnp.float32)
    zonal_branch = (branch_flags % 3).astype(jnp.float32) * 0.5
    merid_branch = (branch_flags // 3).astype(jnp.float32) * 0.5
    east_self = sea[None] * (east_speed[None] * (1.0 - zonal_branch) + diffusion)
    east_next = sea[None] * (east_speed[None] * zonal_branch - diffusion)
    north_self = sea[None] * (north_speed[None] * (1.0 - merid_branch) + diffusion)
    north_next = sea[None] * (north_speed[None] * merid_branch - diffusion)
    lon_coef = jnp.concatenate([sea[None], east_next], axis=0)
    lat_coef = jnp.concatenate([sea[None], north_next], axis=0)
    global_rows = rows * lax.axis_size("lat")
    row_index = lax.axis_index("lat") * rows + jnp.arange(rows)
    coriolis = (0.2 + 0.6 * (row_index.astype(jnp.float32) + 0.5) / global_rows)[None, :, None]
    edge = (levels - 1) * (1 - lax.axis_index("depth"))
    scale = jnp.array([advect_scale, advect_scale, 1.0, 1.0], jnp.float32)[:, None, None, None]
    triangle = (jnp.arange(levels)[None, :] >= jnp.arange(levels)[:, None]).astype(jnp.float32)
    state = jnp.stack([adj_temp, adj_salt, adj_zonal, adj_merid])
    for step_index in reversed(range(STEPS)):
        first = step_index == STEPS - 1
        projected = project(state, block_inverse)
        spike_row, corner, plane = interface(projected, block_inverse, edge)
        other_plane, other_corner = partner((plane, corner), "depth", 0)
        solved = finish(projected, spike_row, corner, plane, other_corner, other_plane, coupling)
        weighted = sea[None] * solved
        outgoing = scale * weighted
        lon_payload = jnp.concatenate([outgoing, lon_coef], axis=0) if first else outgoing
        lat_payload = jnp.concatenate([outgoing, lat_coef], axis=0) if first else outgoing
        lon_wide = with_halo(lon_payload, (("lon", 3),), 1, True)
        lat_wide = with_halo(lat_payload, (("lat", 2),), 1, False)
        if first:
            faces = face_terms(lon_wide[4:], lat_wide[4:], east_self, north_self, sea)
        east_own, west_own, north_own, south_own, sea_lon, sea_lat = faces
        lon_rims = lon_wide[:4]
        lat_rims = lat_wide[:4]
        east_part = east_own[step_index] * (
            lon_rims[:2, ..., 2:] - lon_rims[:2, ..., 1:-1]
        ) + west_own[step_index] * (lon_rims[:2, ..., 1:-1] - lon_rims[:2, ..., :-2])
        north_part = north_own[step_index] * (
            lat_rims[:2, :, 2:] - lat_rims[:2, :, 1:-1]
        ) + south_own[step_index] * (lat_rims[:2, :, 1:-1] - lat_rims[:2, :, :-2])
        tracers = weighted[:2] + east_part + north_part
        beside_all = (
            lon_rims[2:, ..., 2:]
            + lon_rims[2:, ..., :-2]
            + lat_rims[2:, :, 2:]
            + lat_rims[2:, :, :-2]
            - 4.0 * weighted[2:]
        )
        zonal = weighted[2] - coriolis * weighted[3] + viscosity * beside_all[0]
        merid = weighted[3] + coriolis * weighted[2] + viscosity * beside_all[1]
        pressure = (
            -0.5
            * pressure_scale
            * (
                lon_rims[2, ..., :-2]
                - lon_rims[2, ..., 2:]
                + lat_rims[3, :, :-2]
                - lat_rims[3, :, 2:]
            )
        )
        below = jnp.einsum("kj,jyx->kyx", triangle, pressure, precision=lax.Precision.HIGHEST)
        deeper = entering(below[0], "depth", add_sums, jnp.zeros_like(below[0]))
        buoyancy = gravity * (below + deeper[None])
        state = jnp.stack([tracers[0] + buoyancy, tracers[1] - haline * buoyancy, zonal, merid])
    return (state[0], state[1], state[2], state[3])


def solution(mesh):
    in_specs = (
        P("depth", "lat", "lon"),
        P("depth", "lat", "lon"),
        P("depth", "lat", "lon"),
        P("depth", "lat", "lon"),
        P("depth", "lat", "lon"),
        P("depth", "lat", "lon"),
        P(None, "depth", "lat", "lon"),
        P("depth", "lat", "lon"),
        P("lat", "depth", None),
        P("lat"),
    )
    out_specs = (
        P("depth", "lat", "lon"),
        P("depth", "lat", "lon"),
        P("depth", "lat", "lon"),
        P("depth", "lat", "lon"),
    )
    return jax.shard_map(
        on_device, mesh=mesh, in_specs=in_specs, out_specs=out_specs, check_vma=False
    )
```

profile of v0, /device:TPU:32, one launch (start us, length us, event | category | flops | bytes accessed | tf_op | source)
XLA Modules:
  0.0 144.7 jit_solution(4945465144585581292)
XLA Ops:
  0.7 1.1 copy_bitcast_fusion
  1.8 1.1 copy_bitcast_fusion.2
  3.9 15.0 %collective-permute-start = (f32[4,8,128]{2,0,1:T(4,128)S(1)}, f32[4,8,128]{2,0,1:T(4,128)S(1)}, u32[]{:S(2)}, u32[]{:S(2)}) collective-permute-start(f32[4,8,128]{2,0,1:T(4,128)S(1)} %bitcast.136), channel_id=1, source_target_pairs={{0,1},{1,0},{2,3},{3,2},{4,5},{5,4},{6,7},{7,6},{8,9},{9,8},{10,11... | collective-permute-start | bytes 49160 | tf_op jit(solution)/shard_map/ppermute | solution.py:20
  19.1 1.9 %collective-permute-start.1 = (f32[8]{0:T(128)S(1)}, f32[8]{0:T(128)S(1)}, u32[]{:S(2)}, u32[]{:S(2)}) collective-permute-start(f32[8]{0:T(128)S(1)} %dynamic-slice_reduce_fusion), channel_id=1, source_target_pairs={{0,1},{1,0},{2,3},{3,2},{4,5},{5,4},{6,7},{7,6},{8,9},{9,8},{10,11... | collective-permute-start | bytes 104 | tf_op jit(solution)/shard_map/ppermute | solution.py:20
  21.8 11.4 %collective-permute-done.1 = f32[8]{0:T(128)S(1)} collective-permute-done((f32[8]{0:T(128)S(1)}, f32[8]{0:T(128)S(1)}, u32[]{:S(2)}, u32[]{:S(2)}) %collective-permute-start.1) | collective-permute-done | bytes 64 | tf_op jit(solution)/shard_map/ppermute | solution.py:20
  33.5 1.1 fusion.126
  35.7 2.9 %collective-permute-start.4 = (f32[7,48,1,128]{3,1,2,0:T(8,128)}, f32[7,48,1,128]{3,1,2,0:T(8,128)}, u32[]{:S(2)}, u32[]{:S(2)}) collective-permute-start(f32[7,48,1,128]{3,1,2,0:T(8,128)} %get-tuple-element.167), channel_id=1, source_target_pairs={{0,2},{2,4},{4,6},{6,8},{8,10},{10,12},{12,14},{1,3},{3,5},{5,7},{... | collective-permute-start | bytes 516104 | tf_op jit(solution)/shard_map/ppermute | solution.py:30
  38.6 3.6 %collective-permute-start.5 = (f32[7,48,1,128]{3,1,2,0:T(8,128)}, f32[7,48,1,128]{3,1,2,0:T(8,128)}, u32[]{:S(2)}, u32[]{:S(2)}) collective-permute-start(f32[7,48,1,128]{3,1,2,0:T(8,128)} %get-tuple-element.166), channel_id=1, source_target_pairs={{2,0},{4,2},{6,4},{8,6},{10,8},{12,10},{14,12},{3,1},{5,3},{7,5},{... | collective-permute-start | bytes 516104 | tf_op jit(solution)/shard_map/ppermute | solution.py:33
  42.2 1.6 %fusion.122 = (f32[7,48,8,1]{3,1,2,0:T(8,128)S(1)}, f32[7,48,8,1]{3,1,2,0:T(8,128)}) fusion(f32[7,48,8,128]{3,1,2,0:T(8,128)S(1)} %get-tuple-element.172), kind=kLoop, calls=%fused_computation.214 | loop fusion | bytes 43008 | tf_op jit(solution)/shard_map/slice | solution.py:33
  43.8 2.4 %copy.97 = f32[7,48,8,1]{1,2,3,0:T(8,128)} copy(f32[7,48,8,1]{3,1,2,0:T(8,128)} %get-tuple-element.165) | data formatting | bytes 21504 | tf_op jit(solution)/shard_map/slice | solution.py:31
  46.2 1.9 %collective-permute-start.2 = (f32[7,48,8,1]{1,2,3,0:T(8,128)}, f32[7,48,8,1]{1,2,3,0:T(8,128)}, u32[]{:S(2)}, u32[]{:S(2)}) collective-permute-start(f32[7,48,8,1]{1,2,3,0:T(8,128)} %copy.97), channel_id=1, source_target_pairs={{0,16},{16,32},{32,48},{48,64},{64,80},{80,96},{96,112},{112,128},... | collective-permute-start | bytes 32264 | tf_op jit(solution)/shard_map/ppermute | solution.py:30
  48.1 1.1 copy.98
  49.2 7.0 %collective-permute-start.3 = (f32[7,48,8,1]{1,2,3,0:T(8,128)}, f32[7,48,8,1]{1,2,3,0:T(8,128)}, u32[]{:S(2)}, u32[]{:S(2)}) collective-permute-start(f32[7,48,8,1]{1,2,3,0:T(8,128)} %copy.98), channel_id=1, source_target_pairs={{16,0},{32,16},{48,32},{64,48},{80,64},{96,80},{112,96},{128,112},... | collective-permute-start | bytes 32264 | tf_op jit(solution)/shard_map/ppermute | solution.py:33
  56.7 1.6 %copy.93 = f32[48,8,128]{2,0,1:T(8,128)} copy(f32[48,8,128]{2,1,0:T(8,128)} %param.19) | data formatting | bytes 393216 | tf_op args[4]
  58.4 1.6 %copy.103 = f32[48,8,128]{2,0,1:T(8,128)} copy(f32[48,8,128]{2,1,0:T(8,128)} %param.20) | data formatting | bytes 393216 | tf_op args[5]
  60.0 1.2 copy.99
  61.3 2.3 %copy.100 = f32[7,48,8,1]{3,1,2,0:T(8,128)} copy(f32[7,48,8,1]{1,2,3,0:T(8,128)} %collective-permute-done.3) | data formatting | bytes 21504 | tf_op jit(solution)/shard_map/ppermute | solution.py:33
  63.6 1.1 fusion.47
  65.7 1.1 maximum_maximum_fusion
  71.2 1.2 fusion.78
  73.1 13.0 %all_gather.6 = f32[2,8,128]{2,1,0:T(8,128)S(1)} all-gather(f32[1,8,128]{2,1,0:T(8,128)S(1)} %bitcast.140), channel_id=1, replica_groups=mesh['lon'=32,'lat'=8,'depth'=2] {'depth'}, dimensions={0}, use_global_device_ids=true | all-gather | bytes 12288 | tf_op jit(solution)/shard_map/all_gather | solution.py:42
  86.2 1.7 %fusion.36 = f32[2,48,8,128]{3,1,0,2:T(8,128)S(1)} fusion(f32[4,48,8,128]{3,1,0,2:T(8,128)} %copy-done.3, f32[7,48,1,128]{3,1,2,0:T(8,128)} %collective-permute-done.4, f32[2,48,8,128]{3,1,2,0:T(8,128)S(1)} %get-tuple-element.187, f32[1,48,8,128]{3,1,2,0:T(8,128)S(1)} %get-tuple-element.198, f32[4,48,8,128]{3,1,2,0:T(8,128)S(1)} %get-tuple-element.179, ...), kind=kLoop, calls=%fused_computation.62 | loop fusion | flops 1671168 | bytes 2921472 | tf_op jit(solution)/shard_map/sub | solution.py:137
  89.2 1.4 fusion.41
  91.6 2.5 %collective-permute-start.6 = (f32[4,8,128]{2,0,1:T(4,128)S(1)}, f32[4,8,128]{2,0,1:T(4,128)S(1)}, u32[]{:S(2)}, u32[]{:S(2)}) collective-permute-start(f32[4,8,128]{2,0,1:T(4,128)S(1)} %bitcast.138), channel_id=1, source_target_pairs={{0,1},{1,0},{2,3},{3,2},{4,5},{5,4},{6,7},{7,6},{8,9},{9,8},{10,11... | collective-permute-start | bytes 49160 | tf_op jit(solution)/shard_map/ppermute | solution.py:20
  94.1 11.8 %collective-permute-done.6 = f32[4,8,128]{2,0,1:T(4,128)S(1)} collective-permute-done((f32[4,8,128]{2,0,1:T(4,128)S(1)}, f32[4,8,128]{2,0,1:T(4,128)S(1)}, u32[]{:S(2)}, u32[]{:S(2)}) %collective-permute-start.6) | collective-permute-done | bytes 16416 | tf_op jit(solution)/shard_map/ppermute | solution.py:20
  107.0 3.0 %collective-permute-start.10 = (f32[4,48,1,128]{3,1,2,0:T(8,128)}, f32[4,48,1,128]{3,1,2,0:T(8,128)S(1)}, u32[]{:S(2)}, u32[]{:S(2)}) collective-permute-start(f32[4,48,1,128]{3,1,2,0:T(8,128)} %get-tuple-element.177), channel_id=1, source_target_pairs={{0,2},{2,4},{4,6},{6,8},{8,10},{10,12},{12,14},{1,3},{3,5},{5,7},{... | collective-permute-start | bytes 294920 | tf_op jit(solution)/shard_map/ppermute | solution.py:30
  109.9 2.8 %collective-permute-start.9 = (f32[4,48,1,128]{3,1,2,0:T(8,128)}, f32[4,48,1,128]{3,1,2,0:T(8,128)S(1)}, u32[]{:S(2)}, u32[]{:S(2)}) collective-permute-start(f32[4,48,1,128]{3,1,2,0:T(8,128)} %get-tuple-element.176), channel_id=1, source_target_pairs={{2,0},{4,2},{6,4},{8,6},{10,8},{12,10},{14,12},{3,1},{5,3},{7,5},{... | collective-permute-start | bytes 294920 | tf_op jit(solution)/shard_map/ppermute | solution.py:33
  113.4 1.9 %collective-permute-start.8 = (f32[4,48,8,1]{1,2,3,0:T(8,128)S(1)}, f32[4,48,8,1]{1,2,3,0:T(8,128)S(1)}, u32[]{:S(2)}, u32[]{:S(2)}) collective-permute-start(f32[4,48,8,1]{1,2,3,0:T(8,128)S(1)} %copy.118), channel_id=1, source_target_pairs={{0,16},{16,32},{32,48},{48,64},{64,80},{80,96},{96,112},{112,128},... | collective-permute-start | bytes 18440 | tf_op jit(solution)/shard_map/ppermute | solution.py:30
  115.6 7.0 %collective-permute-start.7 = (f32[4,48,8,1]{1,2,3,0:T(8,128)S(1)}, f32[4,48,8,1]{1,2,3,0:T(8,128)}, u32[]{:S(2)}, u32[]{:S(2)}) collective-permute-start(f32[4,48,8,1]{1,2,3,0:T(8,128)S(1)} %copy.116), channel_id=1, source_target_pairs={{16,0},{32,16},{48,32},{64,48},{80,64},{96,80},{112,96},{128,112},... | collective-permute-start | bytes 18440 | tf_op jit(solution)/shard_map/ppermute | solution.py:33
  122.9 1.1 collective-permute-done.7
  126.2 13.0 %all_gather.7 = f32[2,8,128]{2,1,0:T(8,128)S(1)} all-gather(f32[1,8,128]{2,1,0:T(8,128)S(1)} %bitcast.141), channel_id=1, replica_groups=mesh['lon'=32,'lat'=8,'depth'=2] {'depth'}, dimensions={0}, use_global_device_ids=true | all-gather | bytes 12288 | tf_op jit(solution)/shard_map/all_gather | solution.py:42
  139.3 1.6 %fusion.24 = f32[2,48,8,128]{3,1,2,0:T(8,128)S(1)} fusion(f32[4,48,8,128]{3,1,2,0:T(8,128)S(1)} %get-tuple-element.162, f32[4,48,1,128]{3,1,2,0:T(8,128)S(1)} %collective-permute-done.10, f32[4,48,1,128]{3,1,2,0:T(8,128)S(1)} %collective-permute-done.9, f32[4,48,8,1]{3,1,2,0:T(8,128)S(1)} %copy.119, f32[4,48,8,1]{3,1,2,0:T(8,128)S(1)} %copy.117, ...), kind=kLoop, calls=%fused_computation.42 | loop fusion | flops 1572864 | bytes 4521984 | tf_op jit(solution)/shard_map/add | solution.py:135
  (125 shorter events, 19.9 us)
Async XLA Ops:
  0.6 2.3 %copy-start = (f32[8,48,48]{2,1,0:T(8,128)S(1)}, f32[8,48,48]{2,1,0:T(8,128)}, u32[]{:S(2)}) copy-start(f32[8,48,48]{2,1,0:T(8,128)} %param.23) | copy-start | bytes 221188
  1.8 19.2 %copy-start.21 = (s32[48,8,128]{2,1,0:T(8,128)S(1)}, s32[48,8,128]{2,1,0:T(8,128)}, u32[]{:S(2)}) copy-start(s32[48,8,128]{2,1,0:T(8,128)} %param.22) | copy-start | bytes 589828
  2.9 18.1 %copy-start.19 = (f32[48,8,128]{2,1,0:T(8,128)S(1)}, f32[48,8,128]{2,1,0:T(8,128)}, u32[]{:S(2)}) copy-start(f32[48,8,128]{2,1,0:T(8,128)} %param.19) | copy-start | bytes 589828
  3.0 18.2 %copy-start.20 = (f32[48,8,128]{2,1,0:T(8,128)S(1)}, f32[48,8,128]{2,1,0:T(8,128)}, u32[]{:S(2)}) copy-start(f32[48,8,128]{2,1,0:T(8,128)} %param.20) | copy-start | bytes 589828
  3.8 17.4 %copy-start.28 = (f32[8]{0:T(128)S(1)}, f32[8]{0:T(128)}, u32[]{:S(2)}) copy-start(f32[8]{0:T(128)} %param.24) | copy-start | bytes 100
  3.8 17.5 %copy-start.7 = (s32[2,48,8,128]{3,2,1,0:T(8,128)S(1)}, s32[2,48,8,128]{3,2,1,0:T(8,128)}, u32[]{:S(2)}) copy-start(s32[2,48,8,128]{3,2,1,0:T(8,128)} %param.21) | copy-start | bytes 1179652
  3.9 29.3 %collective-permute-start = (f32[4,8,128]{2,0,1:T(4,128)S(1)}, f32[4,8,128]{2,0,1:T(4,128)S(1)}, u32[]{:S(2)}, u32[]{:S(2)}) collective-permute-start(f32[4,8,128]{2,0,1:T(4,128)S(1)} %bitcast.136), channel_id=1, source_target_pairs={{0,1},{1,0},{2,3},{3,2},{4,5},{5,4},{6,7},{7,6},{8,9},{9,8},{10,11... | collective-permute-start | bytes 49160 | tf_op jit(solution)/shard_map/ppermute | solution.py:20
  19.1 14.1 %collective-permute-start.1 = (f32[8]{0:T(128)S(1)}, f32[8]{0:T(128)S(1)}, u32[]{:S(2)}, u32[]{:S(2)}) collective-permute-start(f32[8]{0:T(128)S(1)} %dynamic-slice_reduce_fusion), channel_id=1, source_target_pairs={{0,1},{1,0},{2,3},{3,2},{4,5},{5,4},{6,7},{7,6},{8,9},{9,8},{10,11... | collective-permute-start | bytes 104 | tf_op jit(solution)/shard_map/ppermute | solution.py:20
  21.8 11.7 %copy-start.29 = (f32[4]{0:T(128)S(1)}, f32[4]{0:T(128)}, u32[]{:S(2)}) copy-start(f32[4]{0:T(128)} %constant.134.clone) | copy-start | bytes 52
  33.2 1.4 copy-start.24
  35.7 29.2 %collective-permute-start.4 = (f32[7,48,1,128]{3,1,2,0:T(8,128)}, f32[7,48,1,128]{3,1,2,0:T(8,128)}, u32[]{:S(2)}, u32[]{:S(2)}) collective-permute-start(f32[7,48,1,128]{3,1,2,0:T(8,128)} %get-tuple-element.167), channel_id=1, source_target_pairs={{0,2},{2,4},{4,6},{6,8},{8,10},{10,12},{12,14},{1,3},{3,5},{5,7},{... | collective-permute-start | bytes 516104 | tf_op jit(solution)/shard_map/ppermute | solution.py:30
  38.6 26.3 %collective-permute-start.5 = (f32[7,48,1,128]{3,1,2,0:T(8,128)}, f32[7,48,1,128]{3,1,2,0:T(8,128)}, u32[]{:S(2)}, u32[]{:S(2)}) collective-permute-start(f32[7,48,1,128]{3,1,2,0:T(8,128)} %get-tuple-element.166), channel_id=1, source_target_pairs={{2,0},{4,2},{6,4},{8,6},{10,8},{12,10},{14,12},{3,1},{5,3},{7,5},{... | collective-permute-start | bytes 516104 | tf_op jit(solution)/shard_map/ppermute | solution.py:33
  46.2 13.8 %collective-permute-start.2 = (f32[7,48,8,1]{1,2,3,0:T(8,128)}, f32[7,48,8,1]{1,2,3,0:T(8,128)}, u32[]{:S(2)}, u32[]{:S(2)}) collective-permute-start(f32[7,48,8,1]{1,2,3,0:T(8,128)} %copy.97), channel_id=1, source_target_pairs={{0,16},{16,32},{32,48},{48,64},{64,80},{80,96},{96,112},{112,128},... | collective-permute-start | bytes 32264 | tf_op jit(solution)/shard_map/ppermute | solution.py:30
  49.2 12.0 %collective-permute-start.3 = (f32[7,48,8,1]{1,2,3,0:T(8,128)}, f32[7,48,8,1]{1,2,3,0:T(8,128)}, u32[]{:S(2)}, u32[]{:S(2)}) collective-permute-start(f32[7,48,8,1]{1,2,3,0:T(8,128)} %copy.98), channel_id=1, source_target_pairs={{16,0},{32,16},{48,32},{64,48},{80,64},{96,80},{112,96},{128,112},... | collective-permute-start | bytes 32264 | tf_op jit(solution)/shard_map/ppermute | solution.py:33
  68.9 2.4 %copy-start.1 = (f32[7,48,8,1]{3,1,2,0:T(8,128)S(1)}, f32[7,48,8,1]{3,1,2,0:T(8,128)}, u32[]{:S(2)}) copy-start(f32[7,48,8,1]{3,1,2,0:T(8,128)} %copy.100) | copy-start | bytes 32260
  86.2 1.8 %copy-start.4 = (f32[4,48,8,128]{3,1,0,2:T(8,128)S(1)}, f32[4,48,8,128]{3,1,0,2:T(8,128)}, u32[]{:S(2)}) copy-start(f32[4,48,8,128]{3,1,0,2:T(8,128)} %copy-done.3) | copy-start | bytes 2359300
  86.2 1.8 %copy-start.26 = (f32[8]{0:T(128)S(1)}, f32[8]{0:T(128)}, u32[]{:S(2)}) copy-start(f32[8]{0:T(128)} %multiply_add_fusion) | copy-start | bytes 100
  86.2 1.9 %copy-start.2 = (f32[7,48,8,1]{3,1,2,0:T(8,128)S(1)}, f32[7,48,8,1]{3,1,2,0:T(8,128)}, u32[]{:S(2)}) copy-start(f32[7,48,8,1]{3,1,2,0:T(8,128)} %copy.100) | copy-start | bytes 32260
  86.2 1.9 %copy-start.15 = (f32[48,8,128]{2,0,1:T(8,128)S(1)}, f32[48,8,128]{2,0,1:T(8,128)}, u32[]{:S(2)}) copy-start(f32[48,8,128]{2,0,1:T(8,128)} %get-tuple-element.195) | copy-start | bytes 589828
  86.2 1.9 %copy-start.16 = (f32[48,8,128]{2,0,1:T(8,128)S(1)}, f32[48,8,128]{2,0,1:T(8,128)}, u32[]{:S(2)}) copy-start(f32[48,8,128]{2,0,1:T(8,128)} %get-tuple-element.193) | copy-start | bytes 589828
  86.2 1.9 %copy-start.17 = (f32[48,8,128]{2,0,1:T(8,128)S(1)}, f32[48,8,128]{2,0,1:T(8,128)}, u32[]{:S(2)}) copy-start(f32[48,8,128]{2,0,1:T(8,128)} %get-tuple-element.191) | copy-start | bytes 589828
  86.2 2.0 %copy-start.18 = (f32[48,8,128]{2,0,1:T(8,128)S(1)}, f32[48,8,128]{2,0,1:T(8,128)}, u32[]{:S(2)}) copy-start(f32[48,8,128]{2,0,1:T(8,128)} %get-tuple-element.189) | copy-start | bytes 589828
  89.2 1.4 copy-start.10
  90.6 15.3 %copy-start.23 = (f32[8]{0:T(128)S(1)}, f32[8]{0:T(128)}, u32[]{:S(2)}) copy-start(f32[8]{0:T(128)} %copy-done.22) | copy-start | bytes 100
  90.6 15.3 %copy-start.25 = (f32[8]{0:T(128)S(1)}, f32[8]{0:T(128)}, u32[]{:S(2)}) copy-start(f32[8]{0:T(128)} %copy-done.24) | copy-start | bytes 100
  90.6 15.4 %copy-start.30 = (f32[4]{0:T(128)S(1)}, f32[4]{0:T(128)}, u32[]{:S(2)}) copy-start(f32[4]{0:T(128)} %constant.134.clone) | copy-start | bytes 52
  91.6 14.3 %collective-permute-start.6 = (f32[4,8,128]{2,0,1:T(4,128)S(1)}, f32[4,8,128]{2,0,1:T(4,128)S(1)}, u32[]{:S(2)}, u32[]{:S(2)}) collective-permute-start(f32[4,8,128]{2,0,1:T(4,128)S(1)} %bitcast.138), channel_id=1, source_target_pairs={{0,1},{1,0},{2,3},{3,2},{4,5},{5,4},{6,7},{7,6},{8,9},{9,8},{10,11... | collective-permute-start | bytes 49160 | tf_op jit(solution)/shard_map/ppermute | solution.py:20
  107.0 18.1 %collective-permute-start.10 = (f32[4,48,1,128]{3,1,2,0:T(8,128)}, f32[4,48,1,128]{3,1,2,0:T(8,128)S(1)}, u32[]{:S(2)}, u32[]{:S(2)}) collective-permute-start(f32[4,48,1,128]{3,1,2,0:T(8,128)} %get-tuple-element.177), channel_id=1, source_target_pairs={{0,2},{2,4},{4,6},{6,8},{8,10},{10,12},{12,14},{1,3},{3,5},{5,7},{... | collective-permute-start | bytes 294920 | tf_op jit(solution)/shard_map/ppermute | solution.py:30
  109.9 15.1 %collective-permute-start.9 = (f32[4,48,1,128]{3,1,2,0:T(8,128)}, f32[4,48,1,128]{3,1,2,0:T(8,128)S(1)}, u32[]{:S(2)}, u32[]{:S(2)}) collective-permute-start(f32[4,48,1,128]{3,1,2,0:T(8,128)} %get-tuple-element.176), channel_id=1, source_target_pairs={{2,0},{4,2},{6,4},{8,6},{10,8},{12,10},{14,12},{3,1},{5,3},{7,5},{... | collective-permute-start | bytes 294920 | tf_op jit(solution)/shard_map/ppermute | solution.py:33
  113.4 9.2 %collective-permute-start.8 = (f32[4,48,8,1]{1,2,3,0:T(8,128)S(1)}, f32[4,48,8,1]{1,2,3,0:T(8,128)S(1)}, u32[]{:S(2)}, u32[]{:S(2)}) collective-permute-start(f32[4,48,8,1]{1,2,3,0:T(8,128)S(1)} %copy.118), channel_id=1, source_target_pairs={{0,16},{16,32},{32,48},{48,64},{64,80},{80,96},{96,112},{112,128},... | collective-permute-start | bytes 18440 | tf_op jit(solution)/shard_map/ppermute | solution.py:30
  115.6 8.4 %collective-permute-start.7 = (f32[4,48,8,1]{1,2,3,0:T(8,128)S(1)}, f32[4,48,8,1]{1,2,3,0:T(8,128)}, u32[]{:S(2)}, u32[]{:S(2)}) collective-permute-start(f32[4,48,8,1]{1,2,3,0:T(8,128)S(1)} %copy.116), channel_id=1, source_target_pairs={{16,0},{32,16},{48,32},{64,48},{80,64},{96,80},{112,96},{128,112},... | collective-permute-start | bytes 18440 | tf_op jit(solution)/shard_map/ppermute | solution.py:33
  139.3 1.6 %copy-start.12 = (f32[48,8,128]{2,0,1:T(8,128)S(1)}, f32[48,8,128]{2,0,1:T(8,128)}, u32[]{:S(2)}) copy-start(f32[48,8,128]{2,0,1:T(8,128)} %copy-done.11) | copy-start | bytes 589828
  (10 other events, 10.4 us)
where the time goes:
time: 146 us; the launch traced here: 145 us
  starting transfers between devices  49.5 us (34%)
  local copies, waits for them, and re-layouts  27.9 us (19%)
  blocking collectives  26.1 us (18%)
  waiting for transfers between devices  24.3 us (17%)
  other arithmetic  12.2 us (8%)
  matrix products  3.3 us (2%)
    all_gather x2, blocking collectives, entering(): gathered = lax.all_gather(part, axis)  26.1 us
    ppermute x3, waiting for transfers between devices, partner(): return lax.ppermute(value, axis, pairs)  23.2 us
    ppermute x4, starting transfers between devices, with_halo(): lax.ppermute(lax.slice_in_dim(block, 0, width, axis=dim), axis, backward)  20.3 us
    ppermute x3, starting transfers between devices, partner(): return lax.ppermute(value, axis, pairs)  19.4 us
    ppermute x4, starting transfers between devices, with_halo(): lax.ppermute(lax.slice_in_dim(block, block.shape[dim] - width, None, axis...  9.74 us
    unnamed x68, local copies, waits for them, and re-layouts  9.62 us
    slice x6, local copies, waits for them, and re-layouts, with_halo(): lax.slice_in_dim(block, 0, width, axis=dim)  4.68 us
    ppermute x2, local copies, waits for them, and re-layouts, with_halo(): lax.ppermute(lax.slice_in_dim(block, 0, width, axis=dim), axis, backward)  3.39 us
  transfers between devices with their start and end apart: 11, of which 3 were waited for; matrix products, arithmetic and copies ran while one was open for 12% of the time, Pallas kernels for 0%

commit v1 on v0

v1 whole, which is shorter than its diff:
```python
import functools

import jax
import jax.numpy as jnp
from jax import lax
from jax.experimental import pallas as pl
from jax.experimental.pallas import tpu as pltpu
from jax.sharding import PartitionSpec as P

MESH = pl.DeviceIdType.MESH
F32, BF16, I32 = jnp.float32, jnp.bfloat16, jnp.int32

STEPS = 2
advect_scale = 0.25
diffusion = 0.5
gravity = 0.1
pressure_scale = 1.0
viscosity = 0.1
haline = 0.8

CORNER, PLANE, ZU, ZV, ZS = 0, 1, 5, 6, 7
LOW, HIGH = 0, 1
DEP, LON, LAT, DLON, DLAT, COEF, MISC = 0, 1, 3, 5, 7, 9, 11


def tile(k):
    return pl.ds(pl.multiple_of(k * 8, 8), 8)


def split(value):
    high = value.astype(BF16)
    return high, (value - high.astype(F32)).astype(BF16)


def kernel(
    n_lon, n_lat, lev,
    a_t, a_s, a_u, a_v, es_h, ns_h, fl_h, sea_h, inv_h, coup_h,
    out,
    st, es, ns, fl, sea_i, inv,
    sea, cs, sh, e_own, w_own, n_own, s_own, c0, proj, hx, enh, w3,
    wlat, cs_lat, spike,
    d_s, d_r, lon_s, lon_r, lat_s, lat_r, coef_s, coef_r, misc_s, misc_r, dl_s, dl_r, dt_s, dt_r,
    coup, in_sem, send_sem, recv_sem,
):
    lon, lat, dep = lax.axis_index("lon"), lax.axis_index("lat"), lax.axis_index("depth")
    edge = (lev - 1) * (1 - dep)
    cells = lev * 8
    east, west = lax.rem(lon + 1, n_lon), lax.rem(lon + n_lon - 1, n_lon)
    has_low, has_high = lat > 0, lat < n_lat - 1
    other = 1 - dep

    loads = []
    for i, (src, dst) in enumerate(
        [(inv_h, inv), (a_t, st.at[0]), (a_s, st.at[1]), (a_u, st.at[2]), (a_v, st.at[3]),
         (sea_h, sea_i), (es_h, es), (ns_h, ns), (fl_h, fl), (coup_h, coup)]
    ):
        copy = pltpu.make_async_copy(src, dst, in_sem.at[i])
        copy.start()
        loads.append(copy)

    barrier = pltpu.get_barrier_semaphore()

    def greet(device):
        pl.semaphore_signal(barrier, inc=1, device_id=device, device_id_type=MESH)

    greet((lon, lat, other))
    for depth in (other, dep):
        greet((east, lat, depth))
        greet((west, lat, depth))

        @pl.when(has_low)
        def _():
            greet((lon, lat - 1, depth))

        @pl.when(has_high)
        def _():
            greet((lon, lat + 1, depth))

    lane = lax.broadcasted_iota(I32, (8, 128), 1)
    sub = lax.broadcasted_iota(I32, (8, 128), 0)
    first_lane, last_lane = lane == 0, lane == 127
    first_sub, last_sub = sub == 0, sub == 7
    zero = jnp.zeros((8, 128), F32)

    def to_east(a, halo):
        return jnp.where(last_lane, halo, pltpu.roll(a, 127, 1))

    def to_west(a, halo):
        return jnp.where(first_lane, halo, pltpu.roll(a, 1, 1))

    def to_north(a, halo):
        return jnp.where(last_sub, halo, pltpu.roll(a, 7, 0))

    def to_south(a, halo):
        return jnp.where(first_sub, halo, pltpu.roll(a, 1, 0))

    def copies(step):
        def remote(slot, src, dst, device):
            return pltpu.make_async_remote_copy(
                src_ref=src, dst_ref=dst, send_sem=send_sem.at[step, slot],
                recv_sem=recv_sem.at[step, slot], device_id=device, device_id_type=MESH,
            )

        first = step == 0
        upward = pl.ds(0, 8) if first else pl.ds(1, 6)
        downward = pl.ds(0, 5) if first else pl.ds(1, 4)
        todo = {}
        todo["up"] = (remote(DEP, d_s.at[step, upward], d_r.at[step, upward], (lon, lat, other)), dep == 1, dep == 0)
        todo["down"] = (remote(DEP, d_s.at[step, downward], d_r.at[step, downward], (lon, lat, other)), dep == 0, dep == 1)
        for side in (LOW, HIGH):
            far = 1 - side
            beside = east if side == HIGH else west
            row = lat + 1 if side == HIGH else lat - 1
            sends, gets = (has_high, has_low) if side == HIGH else (has_low, has_high)
            todo["dlon", side] = (remote(DLON + side, dl_s.at[step, side], dl_r.at[step, far], (beside, lat, other)), None, None)
            todo["dlat", side] = (remote(DLAT + side, dt_s.at[step, side], dt_r.at[step, far], (lon, row, other)), sends, gets)
            todo["lon", side] = (remote(LON + side, lon_s.at[step, side], lon_r.at[step, far], (beside, lat, dep)), None, None)
            todo["lat", side] = (remote(LAT + side, lat_s.at[step, side], lat_r.at[step, far], (lon, row, dep)), sends, gets)
            if first:
                count = 3 if side == HIGH else 1
                todo["coef", side] = (
                    remote(COEF + side, coef_s.at[side, pl.ds(0, count)], coef_r.at[far, pl.ds(0, count)], (lon, row, dep)), sends, gets)
                todo["misc", side] = (remote(MISC + side, misc_s, misc_r.at[far], (lon, row, dep)), sends, gets)
        return todo

    def act(entry, what):
        descriptor, sends, gets = entry
        call = {"start": descriptor.start, "send": descriptor.wait_send, "recv": descriptor.wait_recv}[what]
        condition = gets if what == "recv" else sends
        if condition is None:
            call()
        else:
            pl.when(condition)(call)

    for side, missing in ((LOW, lat == 0), (HIGH, lat == n_lat - 1)):

        @pl.when(missing)
        def _():
            for step in range(STEPS):
                lat_r[step, side] = jnp.zeros(lat_r.shape[2:], F32)
                dt_r[step, side] = zero
            coef_r[side] = jnp.zeros(coef_r.shape[1:], F32)
            misc_r[side] = jnp.zeros(misc_r.shape[1:], F32)

    loads[0].wait()
    loads[9].wait()
    coupling = zero
    for y in range(8):
        coupling = jnp.where(sub == y, coup[y], coupling)
    spike[...] = zero
    for y in range(8):
        spike[y : y + 1, 0:lev] = inv[y, pl.ds(edge, 1), :]
        high, low = split(inv[y])
        w3[y] = jnp.concatenate([high, high, low], axis=0)
    spike_rows = spike[...]
    corner = jnp.broadcast_to(
        jnp.sum(jnp.where(lane == edge, spike_rows, 0.0), axis=1, keepdims=True), (8, 128)
    )
    scaled = spike_rows * coupling
    for k in range(lev):
        cs[tile(k)] = jnp.broadcast_to(scaled[:, k : k + 1], (8, 128))
    misc_s[0] = scaled
    misc_s[1] = coupling
    misc_s[2] = corner

    def project(step):
        for y in range(8):
            rows = pl.ds(y, lev, stride=8)
            column = jnp.concatenate([st[f, rows, :] for f in range(4)], axis=1)
            high, low = split(column)
            stacked = jnp.concatenate([high, low, high], axis=0)
            result = lax.dot_general(
                w3[y], stacked, (((0,), (0,)), ((), ())), preferred_element_type=F32
            )
            for f in range(4):
                part = result[:, f * 128 : (f + 1) * 128]
                proj[f, rows, :] = part
                if y == 0:
                    lat_s[step, LOW, f] = part
                if y == 7:
                    lat_s[step, HIGH, f] = part

    for copy in loads[1:5]:
        copy.wait()
    project(0)

    for copy in loads[5:9]:
        copy.wait()

    def prepare(k, carry):
        t = tile(k)
        mask = sea_i[t].astype(F32)
        sea[t] = mask
        quarter = mask * advect_scale
        speed_e, speed_n = es[t], ns[t]
        for n in range(STEPS):
            flag = fl[n, t]
            third = lax.shift_right_logical(flag * 11, 5)
            zonal = (flag - 3 * third).astype(F32) * 0.5
            merid = third.astype(F32) * 0.5
            e_own[n, t] = quarter * (speed_e * (1.0 - zonal) + diffusion)
            w_own[n, t] = quarter * (speed_e * zonal - diffusion)
            n_own[n, t] = quarter * (speed_n * (1.0 - merid) + diffusion)
            s_own[n, t] = quarter * (speed_n * merid - diffusion)
        return carry + mask * cs[t]

    spike_sum = lax.fori_loop(0, lev, prepare, zero, unroll=4)
    d_s[0, CORNER] = corner
    d_s[0, ZS] = spike_sum
    for side, y in ((LOW, 0), (HIGH, 7)):
        rows = pl.ds(y, lev, stride=8)
        coef_s[side, 0] = sea[rows, :]
        if side == HIGH:
            for n in range(STEPS):
                coef_s[side, 1 + n] = s_own[n, rows, :]

    pick_row = lax.broadcasted_iota(I32, (16, 128), 0)
    pick_lane = lax.broadcasted_iota(I32, (16, 128), 1)
    pick_edge = pick_lane == jnp.where(pick_row < 8, 0, 127)

    def messages(step):
        planes = [proj[f, tile(edge)] for f in range(4)]

        def sums(k, carry):
            t = tile(k)
            return carry[0] + sea[t] * proj[2, t], carry[1] + sea[t] * proj[3, t]

        z_u, z_v = lax.fori_loop(0, lev, sums, (zero, zero), unroll=8)
        for f in range(4):
            d_s[step, PLANE + f] = planes[f]
        d_s[step, ZU] = z_u
        d_s[step, ZV] = z_v
        for side, x in ((LOW, 0), (HIGH, 127)):
            packed = zero
            for i, value in enumerate(planes + [z_u, spike_sum]):
                packed = jnp.where(lane == i, jnp.broadcast_to(value[:, x : x + 1], (8, 128)), packed)
            dl_s[step, side] = packed
        for side, y in ((LOW, 0), (HIGH, 7)):
            for i, value in enumerate([corner] + planes + [z_v, spike_sum]):
                dt_s[step, side, i : i + 1, :] = value[y : y + 1, :]
            dt_s[step, side, 7:8, :] = zero[0:1, :]

    def edges(step):
        fields = [proj.at[f] for f in range(4)]
        if step == 0:
            fields = fields + [sea, w_own.at[0], w_own.at[1]]
        total = jnp.zeros((16, cells), F32)
        for i, field in enumerate(fields):
            pick = jnp.where(pick_edge & (lax.rem(pick_row, 8) == i), 1.0, 0.0).astype(BF16)
            for part in split(field[...]):
                total += lax.dot_general(
                    pick, part, (((1,), (1,)), ((), ())), preferred_element_type=F32
                )
        lon_s[step, LOW] = total[0:8]
        lon_s[step, HIGH] = total[8:16]

    def spread(step):
        count = 7 if step == 0 else 4
        parts = []
        for side in (HIGH, LOW):
            value = lon_r[step, side]
            high = value.astype(BF16).astype(F32)
            parts += [high, value - high]
        stacked = jnp.concatenate(parts, axis=0).astype(BF16)
        row = lax.broadcasted_iota(I32, (32, 128), 0)
        at = lax.broadcasted_iota(I32, (32, 128), 1) == jnp.where(row < 16, 127, 0)
        place = jnp.concatenate(
            [jnp.where(at & (lax.rem(row, 8) == i), 1.0, 0.0) for i in range(count)], axis=1
        ).astype(BF16)
        wide = lax.dot_general(stacked, place, (((0,), (0,)), ((), ())), preferred_element_type=F32)
        for i, field in enumerate([hx.at[0], hx.at[1], hx.at[2], hx.at[3], sh, enh.at[0], enh.at[1]][:count]):
            field[...] = wide[:, i * 128 : (i + 1) * 128]

    def faces(k, carry):
        t = tile(k)
        mask, halo = sea[t], sh[t]
        row = pl.ds(k, 1)
        mask_e = to_east(mask, halo)
        mask_n = to_north(mask, coef_r[HIGH, 0, row, :])
        for n in range(STEPS):
            e = e_own[n, t] * mask_e
            w = mask * to_west(w_own[n, t], enh[n, t])
            north = n_own[n, t] * mask_n
            south = mask * to_south(s_own[n, t], coef_r[LOW, 1 + n, row, :])
            e_own[n, t] = e
            w_own[n, t] = w
            n_own[n, t] = north
            s_own[n, t] = south
            c0[n, t] = (1.0 - e + w) - (north - south)
        return carry

    def spread_spikes():
        k_at = lax.broadcasted_iota(I32, (lev, 128), 0)
        same = k_at == lax.broadcasted_iota(I32, (lev, 128), 1)
        for side, y in ((LOW, 7), (HIGH, 0)):
            row = misc_r[side, 0, y : y + 1, :]
            column = jnp.sum(jnp.where(same, jnp.broadcast_to(row, (lev, 128)), 0.0), axis=1, keepdims=True)
            cs_lat[side] = jnp.broadcast_to(column, (lev, 128))

    row_at = (sub + lat * 8).astype(F32)
    coriolis = 0.2 + 0.6 * (row_at + 0.5) / (8.0 * n_lat)

    def advance(step, n, target):
        other_corner = d_r[0, CORNER]
        alpha = 1.0 / (1.0 - coupling * coupling * corner * other_corner)
        beta = coupling * other_corner * alpha
        gamma = coupling * corner * alpha
        own = [proj[f, tile(edge)] for f in range(4)]
        far = [d_r[step, PLANE + f] for f in range(4)]
        carried = [alpha * far[f] + beta * own[f] for f in range(4)]

        def beside(i):
            low = jnp.broadcast_to(dl_r[step, LOW, :, i : i + 1], (8, 128))
            high = jnp.broadcast_to(dl_r[step, HIGH, :, i : i + 1], (8, 128))
            return jnp.where(last_lane, high, jnp.where(first_lane, low, 0.0))

        own_side = [hx[f, tile(edge)] for f in range(4)]
        far_side = [beside(f) for f in range(4)]
        carried_side = [alpha * far_side[f] + beta * own_side[f] for f in range(4)]

        z_u = d_r[step, ZU] + d_r[0, ZS] * (alpha * own[2] + gamma * far[2])
        z_v = d_r[step, ZV] + d_r[0, ZS] * (alpha * own[3] + gamma * far[3])
        z_side = beside(4) + beside(5) * (alpha * own_side[2] + gamma * far_side[2])
        z_rows = []
        for side, y in ((LOW, 7), (HIGH, 0)):
            c = misc_r[side, 1, y : y + 1, :]
            mine = misc_r[side, 2, y : y + 1, :]
            theirs = dt_r[step, side, 0:1, :]
            a = 1.0 / (1.0 - c * c * mine * theirs)
            b = c * theirs * a
            g = c * mine * a
            mask = coef_r[side, 0]
            for f in range(4):
                near = lat_r[step, side, f, pl.ds(edge, 1), :]
                row = dt_r[step, side, 1 + f : 2 + f, :]
                carried_row = a * row + b * near
                wlat[side, f] = mask * (lat_r[step, side, f] + cs_lat[side] * carried_row)
                if f == 3:
                    z_rows.append(dt_r[step, side, 5:6, :] + dt_r[step, side, 6:7, :] * (a * near + g * row))
        deeper = -0.5 * pressure_scale * (
            to_west(z_u, z_side) - to_east(z_u, z_side)
            + to_south(z_v, z_rows[LOW]) - to_north(z_v, z_rows[HIGH])
        )
        deeper = jnp.where(dep == 0, deeper, 0.0)

        def level(i, below):
            k = lev - 1 - i
            t = tile(k)
            row = pl.ds(k, 1)
            mask, tip, halo = sea[t], cs[t], sh[t]
            w, e_, w_, n_, s_ = [], [], [], [], []
            for f in range(4):
                here = mask * (proj[f, t] + tip * carried[f])
                side = halo * (hx[f, t] + tip * carried_side[f])
                w.append(here)
                e_.append(to_east(here, side))
                w_.append(to_west(here, side))
                n_.append(to_north(here, wlat[HIGH, f, row, :]))
                s_.append(to_south(here, wlat[LOW, f, row, :]))
            below = below + (-0.5 * pressure_scale) * (w_[2] - e_[2] + s_[3] - n_[3])
            lift = gravity * below
            ce, cw, cn, cs_, cc = e_own[n, t], w_own[n, t], n_own[n, t], s_own[n, t], c0[n, t]
            for f, part in ((0, lift), (1, -haline * lift)):
                target[f, t] = (cc * w[f] + ce * e_[f]) + (cn * n_[f] - cw * w_[f]) + (part - cs_ * s_[f])
            around = [e_[f] + w_[f] + n_[f] + s_[f] for f in (2, 3)]
            target[2, t] = (1.0 - 4.0 * viscosity) * w[2] - coriolis * w[3] + viscosity * around[0]
            target[3, t] = (1.0 - 4.0 * viscosity) * w[3] + coriolis * w[2] + viscosity * around[1]
            return below

        lax.fori_loop(0, lev, level, deeper, unroll=4)

    messages(0)
    edges(0)
    todo = [copies(0), copies(1)]
    pl.semaphore_wait(barrier, 5 + 2 * has_low.astype(I32) + 2 * has_high.astype(I32))

    for step in range(STEPS):
        now = todo[step]
        if step > 0:
            project(step)
            messages(step)
        order = ["up", "down"] + [(kind, side) for kind in ("dlat", "dlon") for side in (LOW, HIGH)]
        for name in order:
            act(now[name], "start")
        if step > 0:
            edges(step)
        rest = [(kind, side) for kind in ("lon", "misc", "coef", "lat") for side in (LOW, HIGH)]
        for name in rest:
            if name in now:
                act(now[name], "start")
        for name in rest:
            if name in now:
                act(now[name], "recv")
        spread(step)
        if step == 0:
            spread_spikes()
            lax.fori_loop(0, lev, faces, 0, unroll=4)
        for name in order:
            act(now[name], "recv")
        advance(step, STEPS - 1 - step, st if step < STEPS - 1 else out)
    for now in todo:
        for entry in now.values():
            act(entry, "send")


def store(state, *rest):
    outs, sem = rest[:4], rest[4]
    moves = [pltpu.make_async_copy(state.at[f], outs[f], sem.at[f]) for f in range(4)]
    for move in moves:
        move.start()
    for move in moves:
        move.wait()


def on_device(
    n_lon, n_lat,
    adj_temp, adj_salt, adj_zonal, adj_merid, east_speed, north_speed, branch_flags, sea_mask, block_inverse, coupling,
):
    lev, rows, cols = adj_temp.shape
    cells = lev * rows
    flat = [v.reshape(cells, cols) for v in (adj_temp, adj_salt, adj_zonal, adj_merid, east_speed, north_speed)]
    flags = branch_flags.reshape(STEPS, cells, cols)
    hbm = pl.BlockSpec(memory_space=pltpu.HBM)
    anywhere = pl.BlockSpec(memory_space=pl.ANY)
    vmem = pl.BlockSpec(memory_space=pltpu.VMEM)
    field = pltpu.VMEM((cells, cols), F32)

    def fields(*lead):
        return pltpu.VMEM((*lead, cells, cols), F32)

    def tiles(*lead):
        return pltpu.VMEM((*lead, 8, 128), F32)

    scratch = [
        fields(4), field, field, pltpu.VMEM((STEPS, cells, cols), I32), pltpu.VMEM((cells, cols), I32),
        pltpu.VMEM((rows, lev, lev), F32),
        field, field, field,
        fields(STEPS), fields(STEPS), fields(STEPS), fields(STEPS), fields(STEPS),
        fields(4), fields(4), fields(STEPS), pltpu.VMEM((rows, 3 * lev, lev), BF16),
        pltpu.VMEM((2, 4, lev, 128), F32), pltpu.VMEM((2, lev, 128), F32), tiles(),
        tiles(STEPS, 8), tiles(STEPS, 8),
        pltpu.VMEM((STEPS, 2, 8, cells), F32), pltpu.VMEM((STEPS, 2, 8, cells), F32),
        pltpu.VMEM((STEPS, 2, 4, lev, 128), F32), pltpu.VMEM((STEPS, 2, 4, lev, 128), F32),
        pltpu.VMEM((2, 3, lev, 128), F32), pltpu.VMEM((2, 3, lev, 128), F32),
        tiles(3), tiles(2, 3),
        tiles(STEPS, 2), tiles(STEPS, 2), tiles(STEPS, 2), tiles(STEPS, 2),
        pltpu.SMEM((rows,), F32), pltpu.SemaphoreType.DMA((10,)),
        pltpu.SemaphoreType.DMA((STEPS, 13)), pltpu.SemaphoreType.DMA((STEPS, 13)),
    ]
    state = pl.pallas_call(
        functools.partial(kernel, n_lon, n_lat, lev),
        out_shape=jax.ShapeDtypeStruct((4, cells, cols), F32),
        in_specs=[hbm] * 10,
        out_specs=vmem,
        scratch_shapes=scratch,
        compiler_params=pltpu.CompilerParams(
            collective_id=0, has_side_effects=True, vmem_limit_bytes=56 * 1024 * 1024
        ),
        name="adjoint",
    )(*flat, flags, sea_mask.reshape(cells, cols), block_inverse, coupling)
    grads = pl.pallas_call(
        store,
        out_shape=[jax.ShapeDtypeStruct((cells, cols), F32)] * 4,
        in_specs=[anywhere],
        out_specs=[hbm] * 4,
        scratch_shapes=[pltpu.SemaphoreType.DMA((4,))],
        compiler_params=pltpu.CompilerParams(vmem_limit_bytes=8 * 1024 * 1024),
        name="store",
    )(state)
    return tuple(g.reshape(lev, rows, cols) for g in grads)


def solution(mesh):
    field = P("depth", "lat", "lon")
    in_specs = (field,) * 6 + (P(None, "depth", "lat", "lon"), field, P("lat", "depth", None), P("lat"))
    return jax.shard_map(
        functools.partial(on_device, mesh.shape["lon"], mesh.shape["lat"]),
        mesh=mesh,
        in_specs=in_specs,
        out_specs=(field,) * 4,
        check_vma=False,
    )
```

time: 146 us -> 44.3 us (0.30)
  starting transfers between devices: 49.5 us -> 0 us
  Pallas kernels: 0 us -> 42.2 us
  local copies, waits for them, and re-layouts: 27.9 us -> 1.13 us
  blocking collectives: 26.1 us -> 0 us
  waiting for transfers between devices: 24.3 us -> 0 us
  other arithmetic: 12.2 us -> 0 us
  matrix products: 3.3 us -> 0 us
    ppermute x11 -> x0, starting transfers between devices: 49.5 us -> none  [the longest x4 20.3 us: with_halo(): lax.ppermute(lax.slice_in_dim(block, 0, width, axis=dim), axis, backward)]
    pallas_call x0 -> x2, Pallas kernels: none -> 42.2 us  [the longest x1 41.3 us: on_device(): pl.pallas_call(functools.partial(kernel, n_lon, n_lat, lev), out_shape=ja...]
    all_gather x2 -> x0, blocking collectives: 26.1 us -> none  [entering(): gathered = lax.all_gather(part, axis)]
    ppermute x11 -> x0, waiting for transfers between devices: 24.3 us -> none  [the longest x3 23.2 us: partner(): return lax.ppermute(value, axis, pairs)]
    unnamed x68 -> x2, local copies, waits for them, and re-layouts: 9.62 us -> 1.13 us
    slice x12 -> x0, local copies, waits for them, and re-layouts: 7.54 us -> none  [the longest x6 4.68 us: with_halo(): lax.slice_in_dim(block, 0, width, axis=dim)]
    ppermute x4 -> x0, local copies, waits for them, and re-layouts: 4.97 us -> none  [the longest x2 3.39 us: with_halo(): lax.ppermute(lax.slice_in_dim(block, 0, width, axis=dim), axis, backward)]
    add x7 -> x0, other arithmetic: 3.84 us -> none  [the longest x2 3.05 us: on_device(): tracers = weighted[:2] + east_part + north_part]
  transfers between devices with their start and end apart: 11 -> 0, of which waited for: 3 -> 0; matrix products, arithmetic and copies ran while one was open for 12% -> 0% of each run, Pallas kernels for 0% -> 0%
where the time goes in v1:
time: 44.3 us; the launch traced here: 44 us
  Pallas kernels  42.2 us (95%)
  local copies, waits for them, and re-layouts  1.13 us (3%)
  between operations  0.65 us (1%)
    pallas_call x1, Pallas kernels, on_device(): pl.pallas_call(functools.partial(kernel, n_lon, n_lat, lev), out_shape=ja...  41.3 us
    unnamed x2, local copies, waits for them, and re-layouts  1.13 us
    pallas_call x1, Pallas kernels, on_device(): pl.pallas_call(store, out_shape=[jax.ShapeDtypeStruct((cells, cols), F32)...  0.9 us

profile of v1, /device:TPU:32, one launch (start us, length us, event | category | flops | bytes accessed | tf_op | source)
XLA Modules:
  0.0 44.0 jit_solution(1848848019230291590)
XLA Ops:
  0.6 41.3 %adjoint.1.state = f32[4,384,128]{2,1,0:T(8,128)} custom-call(f32[384,128]{1,0:T(8,128)} %bitcast.13, f32[384,128]{1,0:T(8,128)} %bitcast.14, f32[384,128]{1,0:T(8,128)} %bitcast.15, f32[384,128]{1,0:T(8,128)} %bitcast.16, f32[384,128]{1,0:T(8,128)} %bitcast.17, f32[384,128]{1,0:T(8,128)} %bitcast.18, s32[2,384,128]{2,1,0:T(8,128)} %bitcast.12, ...), custom_call_target="tpu_custom_call" | custom-call | tf_op jit(solution)/shard_map/adjoint/pallas_call | solution.py:450
  41.9 0.0 copy-start
  42.0 1.1 %copy-done = f32[4,384,128]{2,1,0:T(8,128)S(1)} copy-done((f32[4,384,128]{2,1,0:T(8,128)S(1)}, f32[4,384,128]{2,1,0:T(8,128)}, u32[]{:S(2)}) %copy-start) | copy-done | bytes 786456
  43.1 0.9 %store.1 = (f32[384,128]{1,0:T(8,128)}, f32[384,128]{1,0:T(8,128)}, f32[384,128]{1,0:T(8,128)}, f32[384,128]{1,0:T(8,128)}) custom-call(f32[4,384,128]{2,1,0:T(8,128)S(1)} %copy-done), custom_call_target="tpu_custom_call" | custom-call | tf_op jit(solution)/shard_map/store/pallas_call | solution.py:461
Async XLA Ops:
  41.9 1.1 %copy-start = (f32[4,384,128]{2,1,0:T(8,128)S(1)}, f32[4,384,128]{2,1,0:T(8,128)}, u32[]{:S(2)}) copy-start(f32[4,384,128]{2,1,0:T(8,128)} %adjoint.1.state) | copy-start | bytes 2359300

commit v2 on v1

--- a/solution.py
+++ b/solution.py
@@ -38,7 +38,7 @@
     out,
     st, es, ns, fl, sea_i, inv,
     sea, cs, sh, e_own, w_own, n_own, s_own, c0, proj, hx, enh, w3,
-    wlat, cs_lat, spike,
+    wlat, cs_lat, spike, q, pc,
     d_s, d_r, lon_s, lon_r, lat_s, lat_r, coef_s, coef_r, misc_s, misc_r, dl_s, dl_r, dt_s, dt_r,
     coup, in_sem, send_sem, recv_sem,
 ):
@@ -49,6 +49,25 @@
     has_low, has_high = lat > 0, lat < n_lat - 1
     other = 1 - dep
 
+    barrier = pltpu.get_barrier_semaphore()
+
+    def greet(device):
+        pl.semaphore_signal(barrier, inc=1, device_id=device, device_id_type=MESH)
+
+    for depth in (other, dep):
+        greet((east, lat, depth))
+        greet((west, lat, depth))
+        if depth is other:
+            greet((lon, lat, other))
+
+        @pl.when(has_low)
+        def _():
+            greet((lon, lat - 1, depth))
+
+        @pl.when(has_high)
+        def _():
+            greet((lon, lat + 1, depth))
+
     loads = []
     for i, (src, dst) in enumerate(
         [(inv_h, inv), (a_t, st.at[0]), (a_s, st.at[1]), (a_u, st.at[2]), (a_v, st.at[3]),
@@ -57,24 +76,6 @@
         copy = pltpu.make_async_copy(src, dst, in_sem.at[i])
         copy.start()
         loads.append(copy)
-
-    barrier = pltpu.get_barrier_semaphore()
-
-    def greet(device):
-        pl.semaphore_signal(barrier, inc=1, device_id=device, device_id_type=MESH)
-
-    greet((lon, lat, other))
-    for depth in (other, dep):
-        greet((east, lat, depth))
-        greet((west, lat, depth))
-
-        @pl.when(has_low)
-        def _():
-            greet((lon, lat - 1, depth))
-
-        @pl.when(has_high)
-        def _():
-            greet((lon, lat + 1, depth))
 
     lane = lax.broadcasted_iota(I32, (8, 128), 1)
     sub = lax.broadcasted_iota(I32, (8, 128), 0)
@@ -152,6 +153,9 @@
         spike[y : y + 1, 0:lev] = inv[y, pl.ds(edge, 1), :]
         high, low = split(inv[y])
         w3[y] = jnp.concatenate([high, high, low], axis=0)
+        at_edge = lax.broadcasted_iota(I32, (lev, lev), 1) == edge
+        column = jnp.sum(jnp.where(at_edge, inv[y], 0.0), axis=1, keepdims=True)
+        pc[pl.ds(y, lev, stride=8), :] = jnp.broadcast_to(column, (lev, 128))
     spike_rows = spike[...]
     corner = jnp.broadcast_to(
         jnp.sum(jnp.where(lane == edge, spike_rows, 0.0), axis=1, keepdims=True), (8, 128)
@@ -214,18 +218,26 @@
             for n in range(STEPS):
                 coef_s[side, 1 + n] = s_own[n, rows, :]
 
+    for y in range(8):
+        rows = pl.ds(y, lev, stride=8)
+        ones = sea[rows, :].astype(BF16)
+        high, low = split(inv[y])
+        q[rows, :] = jnp.dot(high, ones, preferred_element_type=F32) + jnp.dot(low, ones, preferred_element_type=F32)
+
     pick_row = lax.broadcasted_iota(I32, (16, 128), 0)
     pick_lane = lax.broadcasted_iota(I32, (16, 128), 1)
     pick_edge = pick_lane == jnp.where(pick_row < 8, 0, 127)
 
-    def messages(step):
-        planes = [proj[f, tile(edge)] for f in range(4)]
-
+    def first_sums():
         def sums(k, carry):
             t = tile(k)
             return carry[0] + sea[t] * proj[2, t], carry[1] + sea[t] * proj[3, t]
 
-        z_u, z_v = lax.fori_loop(0, lev, sums, (zero, zero), unroll=8)
+        both = lax.fori_loop(0, lev, sums, (zero, zero), unroll=8)
+        return [proj[f, tile(edge)] for f in range(4)] + list(both)
+
+    def messages(step, sent):
+        planes, z_u, z_v = list(sent[:4]), sent[4], sent[5]
         for f in range(4):
             d_s[step, PLANE + f] = planes[f]
         d_s[step, ZU] = z_u
@@ -343,7 +355,8 @@
         )
         deeper = jnp.where(dep == 0, deeper, 0.0)
 
-        def level(i, below):
+        def level(i, carry):
+            below, sent = carry[0], list(carry[1:])
             k = lev - 1 - i
             t = tile(k)
             row = pl.ds(k, 1)
@@ -360,16 +373,27 @@
             below = below + (-0.5 * pressure_scale) * (w_[2] - e_[2] + s_[3] - n_[3])
             lift = gravity * below
             ce, cw, cn, cs_, cc = e_own[n, t], w_own[n, t], n_own[n, t], s_own[n, t], c0[n, t]
-            for f, part in ((0, lift), (1, -haline * lift)):
-                target[f, t] = (cc * w[f] + ce * e_[f]) + (cn * n_[f] - cw * w_[f]) + (part - cs_ * s_[f])
-            around = [e_[f] + w_[f] + n_[f] + s_[f] for f in (2, 3)]
-            target[2, t] = (1.0 - 4.0 * viscosity) * w[2] - coriolis * w[3] + viscosity * around[0]
-            target[3, t] = (1.0 - 4.0 * viscosity) * w[3] + coriolis * w[2] + viscosity * around[1]
-            return below
-
-        lax.fori_loop(0, lev, level, deeper, unroll=4)
-
-    messages(0)
+            new = [
+                (cc * w[f] + ce * e_[f]) + (cn * n_[f] - cw * w_[f]) + (part - cs_ * s_[f])
+                for f, part in ((0, lift), (1, -haline * lift))
+            ]
+            for f, turn in ((2, -coriolis * w[3]), (3, coriolis * w[2])):
+                around = (e_[f] + w_[f]) + (n_[f] + s_[f])
+                new.append((1.0 - 4.0 * viscosity) * w[f] + turn + viscosity * around)
+            for f in range(4):
+                target[f, t] = new[f]
+            if sent:
+                weight, mass = pc[t], q[t]
+                for f in range(4):
+                    sent[f] = sent[f] + weight * new[f]
+                sent[4] = sent[4] + mass * new[2]
+                sent[5] = sent[5] + mass * new[3]
+            return (below, *sent)
+
+        following = (zero,) * 6 if step < STEPS - 1 else ()
+        return lax.fori_loop(0, lev, level, (deeper, *following), unroll=8)[1:]
+
+    messages(0, first_sums())
     edges(0)
     todo = [copies(0), copies(1)]
     pl.semaphore_wait(barrier, 5 + 2 * has_low.astype(I32) + 2 * has_high.astype(I32))
@@ -377,12 +401,12 @@
     for step in range(STEPS):
         now = todo[step]
         if step > 0:
-            project(step)
-            messages(step)
-        order = ["up", "down"] + [(kind, side) for kind in ("dlat", "dlon") for side in (LOW, HIGH)]
+            messages(step, sent)
+        order = [("dlon", side) for side in (LOW, HIGH)] + ["up", "down"] + [("dlat", side) for side in (LOW, HIGH)]
         for name in order:
             act(now[name], "start")
         if step > 0:
+            project(step)
             edges(step)
         rest = [(kind, side) for kind in ("lon", "misc", "coef", "lat") for side in (LOW, HIGH)]
         for name in rest:
@@ -397,7 +421,7 @@
             lax.fori_loop(0, lev, faces, 0, unroll=4)
         for name in order:
             act(now[name], "recv")
-        advance(step, STEPS - 1 - step, st if step < STEPS - 1 else out)
+        sent = advance(step, STEPS - 1 - step, st if step < STEPS - 1 else out)
     for now in todo:
         for entry in now.values():
             act(entry, "send")
@@ -437,7 +461,7 @@
         field, field, field,
         fields(STEPS), fields(STEPS), fields(STEPS), fields(STEPS), fields(STEPS),
         fields(4), fields(4), fields(STEPS), pltpu.VMEM((rows, 3 * lev, lev), BF16),
-        pltpu.VMEM((2, 4, lev, 128), F32), pltpu.VMEM((2, lev, 128), F32), tiles(),
+        pltpu.VMEM((2, 4, lev, 128), F32), pltpu.VMEM((2, lev, 128), F32), tiles(), field, field,
         tiles(STEPS, 8), tiles(STEPS, 8),
         pltpu.VMEM((STEPS, 2, 8, cells), F32), pltpu.VMEM((STEPS, 2, 8, cells), F32),
         pltpu.VMEM((STEPS, 2, 4, lev, 128), F32), pltpu.VMEM((STEPS, 2, 4, lev, 128), F32),
@@ -454,10 +478,10 @@
         out_specs=vmem,
         scratch_shapes=scratch,
         compiler_params=pltpu.CompilerParams(
-            collective_id=0, has_side_effects=True, vmem_limit_bytes=56 * 1024 * 1024
+            collective_id=0, has_side_effects=True, vmem_limit_bytes=40 * 1024 * 1024
         ),
         name="adjoint",
-    )(*flat, flags, sea_mask.reshape(cells, cols), block_inverse, coupling)
+    )(*[pltpu.with_memory_space_constraint(v, pltpu.HBM) for v in (*flat, flags, sea_mask.reshape(cells, cols), block_inverse, coupling)])
     grads = pl.pallas_call(
         store,
         out_shape=[jax.ShapeDtypeStruct((cells, cols), F32)] * 4,

time: 44.3 us -> 39.7 us (0.90)
  Pallas kernels: 42.2 us -> 38.9 us
  local copies, waits for them, and re-layouts: 1.13 us -> 0 us
    pallas_call x1, Pallas kernels: 41.3 us -> 38 us  [on_device(): pl.pallas_call(functools.partial(kernel, n_lon, n_lat, lev), out_shape=ja...]
    unnamed x2 -> x0, local copies, waits for them, and re-layouts: 1.13 us -> none
where the time goes in v2:
time: 39.7 us; the launch traced here: 39.6 us
  Pallas kernels  38.9 us (98%)
  between operations  0.64 us (2%)
    pallas_call x1, Pallas kernels, on_device(): pl.pallas_call(functools.partial(kernel, n_lon, n_lat, lev), out_shape=ja...  38 us
    pallas_call x1, Pallas kernels, on_device(): pl.pallas_call(store, out_shape=[jax.ShapeDtypeStruct((cells, cols), F32)...  0.91 us

profile of v2, /device:TPU:32, one launch (start us, length us, event | category | flops | bytes accessed | tf_op | source)
XLA Modules:
  0.0 39.6 jit_solution(16356224863573033123)
XLA Ops:
  0.6 38.0 %adjoint.1.state = f32[4,384,128]{2,1,0:T(8,128)S(1)} custom-call(f32[384,128]{1,0:T(8,128)} %bitcast.13, f32[384,128]{1,0:T(8,128)} %bitcast.14, f32[384,128]{1,0:T(8,128)} %bitcast.15, f32[384,128]{1,0:T(8,128)} %bitcast.16, f32[384,128]{1,0:T(8,128)} %bitcast.17, f32[384,128]{1,0:T(8,128)} %bitcast.18, s32[2,384,128]{2,1,0:T(8,128)} %bitcast.12, ...), custom_call_target="tpu_custom_call" | custom-call | tf_op jit(solution)/shard_map/adjoint/pallas_call | solution.py:474
  38.7 0.9 %store.1 = (f32[384,128]{1,0:T(8,128)}, f32[384,128]{1,0:T(8,128)}, f32[384,128]{1,0:T(8,128)}, f32[384,128]{1,0:T(8,128)}) custom-call(f32[4,384,128]{2,1,0:T(8,128)S(1)} %adjoint.1.state), custom_call_target="tpu_custom_call" | custom-call | tf_op jit(solution)/shard_map/store/pallas_call | solution.py:485

commit v3 on v2

--- a/solution.py
+++ b/solution.py
@@ -38,7 +38,7 @@
     out,
     st, es, ns, fl, sea_i, inv,
     sea, cs, sh, e_own, w_own, n_own, s_own, c0, proj, hx, enh, w3,
-    wlat, cs_lat, spike, q, pc,
+    wlat, cs_lat, spike, q, pc, m5,
     d_s, d_r, lon_s, lon_r, lat_s, lat_r, coef_s, coef_r, misc_s, misc_r, dl_s, dl_r, dt_s, dt_r,
     coup, in_sem, send_sem, recv_sem,
 ):
@@ -206,9 +206,9 @@
             w_own[n, t] = quarter * (speed_e * zonal - diffusion)
             n_own[n, t] = quarter * (speed_n * (1.0 - merid) + diffusion)
             s_own[n, t] = quarter * (speed_n * merid - diffusion)
-        return carry + mask * cs[t]
-
-    spike_sum = lax.fori_loop(0, lev, prepare, zero, unroll=4)
+        return carry[0] + mask * cs[t], carry[1] + pc[t]
+
+    spike_sum, pc_sum = lax.fori_loop(0, lev, prepare, (zero, zero), unroll=4)
     d_s[0, CORNER] = corner
     d_s[0, ZS] = spike_sum
     for side, y in ((LOW, 0), (HIGH, 7)):
@@ -283,22 +283,21 @@
         for i, field in enumerate([hx.at[0], hx.at[1], hx.at[2], hx.at[3], sh, enh.at[0], enh.at[1]][:count]):
             field[...] = wide[:, i * 128 : (i + 1) * 128]
 
-    def faces(k, carry):
+    def faces(n, k, carry):
         t = tile(k)
         mask, halo = sea[t], sh[t]
         row = pl.ds(k, 1)
         mask_e = to_east(mask, halo)
         mask_n = to_north(mask, coef_r[HIGH, 0, row, :])
-        for n in range(STEPS):
-            e = e_own[n, t] * mask_e
-            w = mask * to_west(w_own[n, t], enh[n, t])
-            north = n_own[n, t] * mask_n
-            south = mask * to_south(s_own[n, t], coef_r[LOW, 1 + n, row, :])
-            e_own[n, t] = e
-            w_own[n, t] = w
-            n_own[n, t] = north
-            s_own[n, t] = south
-            c0[n, t] = (1.0 - e + w) - (north - south)
+        e = e_own[n, t] * mask_e
+        w = mask * to_west(w_own[n, t], enh[n, t])
+        north = n_own[n, t] * mask_n
+        south = mask * to_south(s_own[n, t], coef_r[LOW, 1 + n, row, :])
+        e_own[n, t] = e
+        w_own[n, t] = w
+        n_own[n, t] = north
+        s_own[n, t] = south
+        c0[n, t] = (1.0 - e + w) - (north - south)
         return carry
 
     def spread_spikes():
@@ -312,7 +311,82 @@
     row_at = (sub + lat * 8).astype(F32)
     coriolis = 0.2 + 0.6 * (row_at + 0.5) / (8.0 * n_lat)
 
-    def advance(step, n, target):
+    def masses():
+        def level(i, carry):
+            k = lev - 1 - i
+            t = tile(k)
+            row = pl.ds(k, 1)
+            here = sea[t] * cs[t]
+            side = sh[t] * cs[t]
+            values = [
+                here, to_east(here, side), to_west(here, side),
+                to_north(here, coef_r[HIGH, 0, row, :] * cs_lat[HIGH, row, :]),
+                to_south(here, coef_r[LOW, 0, row, :] * cs_lat[LOW, row, :]),
+            ]
+            for j in range(5):
+                m5[j, t] = values[j]
+            above, by_plane, by_above, by_mass = carry
+            weight, mass = pc[t], q[t]
+            return (
+                above - weight,
+                tuple(c + weight * v for c, v in zip(by_plane, values)),
+                tuple(c + above * v for c, v in zip(by_above, values[1:])),
+                tuple(c + mass * v for c, v in zip(by_mass, values)),
+            )
+
+        return lax.fori_loop(0, lev, level, (pc_sum, (zero,) * 5, (zero,) * 4, (zero,) * 5), unroll=8)[1:]
+
+    half = 0.5 * pressure_scale
+
+    def base(step, n, target):
+        for side in (LOW, HIGH):
+            for f in range(4):
+                wlat[side, f] = coef_r[side, 0] * lat_r[step, side, f]
+        count = 11 if step < STEPS - 1 else 0
+
+        def level(i, carry):
+            below, sums = carry[0], list(carry[1:])
+            k = lev - 1 - i
+            t = tile(k)
+            row = pl.ds(k, 1)
+            mask, halo = sea[t], sh[t]
+            w, e_, w_, n_, s_ = [], [], [], [], []
+            for f in range(4):
+                here = mask * proj[f, t]
+                side = halo * hx[f, t]
+                w.append(here)
+                e_.append(to_east(here, side))
+                w_.append(to_west(here, side))
+                n_.append(to_north(here, wlat[HIGH, f, row, :]))
+                s_.append(to_south(here, wlat[LOW, f, row, :]))
+            below = below + half * ((e_[2] - w_[2]) + (n_[3] - s_[3]))
+            lift = gravity * below
+            coefs = [c0[n, t], e_own[n, t], -w_own[n, t], n_own[n, t], -s_own[n, t]]
+            new = [
+                (coefs[0] * w[f] + coefs[1] * e_[f]) + (coefs[3] * n_[f] + coefs[2] * w_[f]) + (part + coefs[4] * s_[f])
+                for f, part in ((0, lift), (1, -haline * lift))
+            ]
+            for f, turn in ((2, -coriolis * w[3]), (3, coriolis * w[2])):
+                around = (e_[f] + w_[f]) + (n_[f] + s_[f])
+                new.append((1.0 - 4.0 * viscosity) * w[f] + turn + viscosity * around)
+            for f in range(4):
+                target[f, t] = new[f]
+            coefs = [c * m5[j, t] for j, c in enumerate(coefs)]
+            for ref, c in zip((c0, e_own, w_own, n_own, s_own), coefs):
+                ref[n, t] = c
+            if sums:
+                weight, mass = pc[t], q[t]
+                for f in range(4):
+                    sums[f] = sums[f] + weight * new[f]
+                sums[4] = sums[4] + mass * new[2]
+                sums[5] = sums[5] + mass * new[3]
+                for j in range(5):
+                    sums[6 + j] = sums[6 + j] + weight * coefs[j]
+            return (below, *sums)
+
+        return lax.fori_loop(0, lev, level, (zero,) * (1 + count), unroll=4)[1:]
+
+    def carry_over(step):
         other_corner = d_r[0, CORNER]
         alpha = 1.0 / (1.0 - coupling * coupling * corner * other_corner)
         beta = coupling * other_corner * alpha
@@ -328,70 +402,76 @@
 
         own_side = [hx[f, tile(edge)] for f in range(4)]
         far_side = [beside(f) for f in range(4)]
-        carried_side = [alpha * far_side[f] + beta * own_side[f] for f in range(4)]
+        side = [alpha * far_side[f] + beta * own_side[f] for f in range(4)]
 
         z_u = d_r[step, ZU] + d_r[0, ZS] * (alpha * own[2] + gamma * far[2])
         z_v = d_r[step, ZV] + d_r[0, ZS] * (alpha * own[3] + gamma * far[3])
         z_side = beside(4) + beside(5) * (alpha * own_side[2] + gamma * far_side[2])
-        z_rows = []
-        for side, y in ((LOW, 7), (HIGH, 0)):
-            c = misc_r[side, 1, y : y + 1, :]
-            mine = misc_r[side, 2, y : y + 1, :]
-            theirs = dt_r[step, side, 0:1, :]
+        z_rows, rows = [], []
+        for at, y in ((LOW, 7), (HIGH, 0)):
+            c = misc_r[at, 1, y : y + 1, :]
+            mine = misc_r[at, 2, y : y + 1, :]
+            theirs = dt_r[step, at, 0:1, :]
             a = 1.0 / (1.0 - c * c * mine * theirs)
             b = c * theirs * a
             g = c * mine * a
-            mask = coef_r[side, 0]
-            for f in range(4):
-                near = lat_r[step, side, f, pl.ds(edge, 1), :]
-                row = dt_r[step, side, 1 + f : 2 + f, :]
-                carried_row = a * row + b * near
-                wlat[side, f] = mask * (lat_r[step, side, f] + cs_lat[side] * carried_row)
-                if f == 3:
-                    z_rows.append(dt_r[step, side, 5:6, :] + dt_r[step, side, 6:7, :] * (a * near + g * row))
-        deeper = -0.5 * pressure_scale * (
-            to_west(z_u, z_side) - to_east(z_u, z_side)
-            + to_south(z_v, z_rows[LOW]) - to_north(z_v, z_rows[HIGH])
+            near = [lat_r[step, at, f, pl.ds(edge, 1), :] for f in range(4)]
+            row = [dt_r[step, at, 1 + f : 2 + f, :] for f in range(4)]
+            rows.append([a * row[f] + b * near[f] for f in range(4)])
+            z_rows.append(dt_r[step, at, 5:6, :] + dt_r[step, at, 6:7, :] * (a * near[3] + g * row[3]))
+        deeper = half * (
+            (to_east(z_u, z_side) - to_west(z_u, z_side))
+            + (to_north(z_v, z_rows[HIGH]) - to_south(z_v, z_rows[LOW]))
         )
         deeper = jnp.where(dep == 0, deeper, 0.0)
-
-        def level(i, carry):
-            below, sent = carry[0], list(carry[1:])
-            k = lev - 1 - i
-            t = tile(k)
-            row = pl.ds(k, 1)
-            mask, tip, halo = sea[t], cs[t], sh[t]
-            w, e_, w_, n_, s_ = [], [], [], [], []
-            for f in range(4):
-                here = mask * (proj[f, t] + tip * carried[f])
-                side = halo * (hx[f, t] + tip * carried_side[f])
-                w.append(here)
-                e_.append(to_east(here, side))
-                w_.append(to_west(here, side))
-                n_.append(to_north(here, wlat[HIGH, f, row, :]))
-                s_.append(to_south(here, wlat[LOW, f, row, :]))
-            below = below + (-0.5 * pressure_scale) * (w_[2] - e_[2] + s_[3] - n_[3])
+        around = [
+            (carried[f], to_east(carried[f], side[f]), to_west(carried[f], side[f]),
+             to_north(carried[f], rows[HIGH][f]), to_south(carried[f], rows[LOW][f]))
+            for f in range(4)
+        ]
+        turned = (
+            (1.0 - 4.0 * viscosity) * carried[2] - coriolis * carried[3],
+            (1.0 - 4.0 * viscosity) * carried[3] + coriolis * carried[2],
+        )
+        slow = [[viscosity * v for v in around[2 + f]] for f in range(2)]
+        return around, turned, slow, deeper
+
+    def combine(weights, values):
+        terms = [a * b for a, b in zip(weights, values)]
+        return (terms[0] + terms[1]) + (terms[2] + terms[3]) + sum(terms[4:], zero)
+
+    def next_sums(sums, weights, interface):
+        around, turned, slow, deeper = interface
+        by_plane, by_above, by_mass = weights
+        press = half * (by_above[0] * around[2][1] - by_above[1] * around[2][2] + by_above[2] * around[3][3] - by_above[3] * around[3][4])
+        lift = gravity * (press + pc_sum * deeper)
+        out_sums = [
+            sums[f] + combine(sums[6:11], around[f]) + part for f, part in ((0, lift), (1, -haline * lift))
+        ]
+        for f in range(2):
+            out_sums.append(sums[2 + f] + combine(by_plane, [turned[f]] + slow[f][1:]))
+        for f in range(2):
+            out_sums.append(sums[4 + f] + combine(by_mass, [turned[f]] + slow[f][1:]))
+        return out_sums
+
+    def finish(n, target, interface):
+        around, turned, slow, deeper = interface
+
+        def level(i, below):
+            t = tile(lev - 1 - i)
+            m = [m5[j, t] for j in range(5)]
+            east_u, west_u = m[1] * around[2][1], m[2] * around[2][2]
+            north_v, south_v = m[3] * around[3][3], m[4] * around[3][4]
+            below = below + half * ((east_u - west_u) + (north_v - south_v))
             lift = gravity * below
-            ce, cw, cn, cs_, cc = e_own[n, t], w_own[n, t], n_own[n, t], s_own[n, t], c0[n, t]
-            new = [
-                (cc * w[f] + ce * e_[f]) + (cn * n_[f] - cw * w_[f]) + (part - cs_ * s_[f])
-                for f, part in ((0, lift), (1, -haline * lift))
-            ]
-            for f, turn in ((2, -coriolis * w[3]), (3, coriolis * w[2])):
-                around = (e_[f] + w_[f]) + (n_[f] + s_[f])
-                new.append((1.0 - 4.0 * viscosity) * w[f] + turn + viscosity * around)
-            for f in range(4):
-                target[f, t] = new[f]
-            if sent:
-                weight, mass = pc[t], q[t]
-                for f in range(4):
-                    sent[f] = sent[f] + weight * new[f]
-                sent[4] = sent[4] + mass * new[2]
-                sent[5] = sent[5] + mass * new[3]
-            return (below, *sent)
-
-        following = (zero,) * 6 if step < STEPS - 1 else ()
-        return lax.fori_loop(0, lev, level, (deeper, *following), unroll=8)[1:]
+            coefs = [c0[n, t], e_own[n, t], w_own[n, t], n_own[n, t], s_own[n, t]]
+            target[0, t] = target[0, t] + combine(coefs, around[0]) + lift
+            target[1, t] = target[1, t] + combine(coefs, around[1]) - haline * lift
+            target[2, t] = (target[2, t] + m[0] * turned[0]) + viscosity * (east_u + west_u) + (m[3] * slow[0][3] + m[4] * slow[0][4])
+            target[3, t] = (target[3, t] + m[0] * turned[1]) + viscosity * (north_v + south_v) + (m[1] * slow[1][1] + m[2] * slow[1][2])
+            return below
+
+        lax.fori_loop(0, lev, level, deeper, unroll=8)
 
     messages(0, first_sums())
     edges(0)
@@ -400,28 +480,38 @@
 
     for step in range(STEPS):
         now = todo[step]
-        if step > 0:
-            messages(step, sent)
         order = [("dlon", side) for side in (LOW, HIGH)] + ["up", "down"] + [("dlat", side) for side in (LOW, HIGH)]
-        for name in order:
-            act(now[name], "start")
-        if step > 0:
+        if step == 0:
+            for name in order:
+                act(now[name], "start")
+        else:
             project(step)
             edges(step)
         rest = [(kind, side) for kind in ("lon", "misc", "coef", "lat") for side in (LOW, HIGH)]
         for name in rest:
             if name in now:
                 act(now[name], "start")
+        if step > 0:
+            lax.fori_loop(0, lev, functools.partial(faces, STEPS - 1 - step), 0, unroll=8)
         for name in rest:
             if name in now:
                 act(now[name], "recv")
         spread(step)
         if step == 0:
             spread_spikes()
-            lax.fori_loop(0, lev, faces, 0, unroll=4)
+            lax.fori_loop(0, lev, functools.partial(faces, STEPS - 1), 0, unroll=8)
+            weights = masses()
+        n = STEPS - 1 - step
+        target = st if step < STEPS - 1 else out
+        sums = base(step, n, target)
         for name in order:
             act(now[name], "recv")
-        sent = advance(step, STEPS - 1 - step, st if step < STEPS - 1 else out)
+        interface = carry_over(step)
+        if step < STEPS - 1:
+            messages(step + 1, next_sums(sums, weights, interface))
+            for name in order:
+                act(todo[step + 1][name], "start")
+        finish(n, target, interface)
     for now in todo:
         for entry in now.values():
             act(entry, "send")
@@ -461,7 +551,7 @@
         field, field, field,
         fields(STEPS), fields(STEPS), fields(STEPS), fields(STEPS), fields(STEPS),
         fields(4), fields(4), fields(STEPS), pltpu.VMEM((rows, 3 * lev, lev), BF16),
-        pltpu.VMEM((2, 4, lev, 128), F32), pltpu.VMEM((2, lev, 128), F32), tiles(), field, field,
+        pltpu.VMEM((2, 4, lev, 128), F32), pltpu.VMEM((2, lev, 128), F32), tiles(), field, field, fields(5),
         tiles(STEPS, 8), tiles(STEPS, 8),
         pltpu.VMEM((STEPS, 2, 8, cells), F32), pltpu.VMEM((STEPS, 2, 8, cells), F32),
         pltpu.VMEM((STEPS, 2, 4, lev, 128), F32), pltpu.VMEM((STEPS, 2, 4, lev, 128), F32),

time: 39.7 us -> 38.4 us (0.967)
  the two profiles are of different devices: /device:TPU:32 before, /device:TPU:55 now
where the time goes in v3:
time: 38.4 us; the launch traced here: 38.2 us
  Pallas kernels  37.6 us (98%)
  between operations  0.64 us (2%)
    pallas_call x1, Pallas kernels, on_device(): pl.pallas_call(functools.partial(kernel, n_lon, n_lat, lev), out_shape=ja...  36.7 us
    pallas_call x1, Pallas kernels, on_device(): pl.pallas_call(store, out_shape=[jax.ShapeDtypeStruct((cells, cols), F32)...  0.91 us

profile of v3, /device:TPU:55, one launch (start us, length us, event | category | flops | bytes accessed | tf_op | source)
XLA Modules:
  0.0 38.2 jit_solution(15336222683170914112)
XLA Ops:
  0.6 36.7 %adjoint.1.state = f32[4,384,128]{2,1,0:T(8,128)S(1)} custom-call(f32[384,128]{1,0:T(8,128)} %bitcast.13, f32[384,128]{1,0:T(8,128)} %bitcast.14, f32[384,128]{1,0:T(8,128)} %bitcast.15, f32[384,128]{1,0:T(8,128)} %bitcast.16, f32[384,128]{1,0:T(8,128)} %bitcast.17, f32[384,128]{1,0:T(8,128)} %bitcast.18, s32[2,384,128]{2,1,0:T(8,128)} %bitcast.12, ...), custom_call_target="tpu_custom_call" | custom-call | tf_op jit(solution)/shard_map/adjoint/pallas_call | solution.py:564
  37.3 0.9 %store.1 = (f32[384,128]{1,0:T(8,128)}, f32[384,128]{1,0:T(8,128)}, f32[384,128]{1,0:T(8,128)}, f32[384,128]{1,0:T(8,128)}) custom-call(f32[4,384,128]{2,1,0:T(8,128)S(1)} %adjoint.1.state), custom_call_target="tpu_custom_call" | custom-call | tf_op jit(solution)/shard_map/store/pallas_call | solution.py:575

commit v4 on v3

--- a/solution.py
+++ b/solution.py
@@ -487,13 +487,13 @@
         else:
             project(step)
             edges(step)
-        rest = [(kind, side) for kind in ("lon", "misc", "coef", "lat") for side in (LOW, HIGH)]
+        rest = [(kind, side) for kind in ("misc", "coef", "lon", "lat") for side in (LOW, HIGH)]
         for name in rest:
             if name in now:
                 act(now[name], "start")
         if step > 0:
             lax.fori_loop(0, lev, functools.partial(faces, STEPS - 1 - step), 0, unroll=8)
-        for name in rest:
+        for name in rest[:-2]:
             if name in now:
                 act(now[name], "recv")
         spread(step)
@@ -501,6 +501,8 @@
             spread_spikes()
             lax.fori_loop(0, lev, functools.partial(faces, STEPS - 1), 0, unroll=8)
             weights = masses()
+        for name in rest[-2:]:
+            act(now[name], "recv")
         n = STEPS - 1 - step
         target = st if step < STEPS - 1 else out
         sums = base(step, n, target)

time: 38.4 us -> 38.3 us (level)
  the two profiles are of different devices: /device:TPU:55 before, /device:TPU:32 now
where the time goes in v4:
time: 38.3 us; the launch traced here: 38.2 us
  Pallas kernels  37.5 us (98%)
  between operations  0.64 us (2%)
    pallas_call x1, Pallas kernels, on_device(): pl.pallas_call(functools.partial(kernel, n_lon, n_lat, lev), out_shape=ja...  36.6 us
    pallas_call x1, Pallas kernels, on_device(): pl.pallas_call(store, out_shape=[jax.ShapeDtypeStruct((cells, cols), F32)...  0.91 us

profile of v4, /device:TPU:32, one launch (start us, length us, event | category | flops | bytes accessed | tf_op | source)
XLA Modules:
  0.0 38.2 jit_solution(8702529394257386981)
XLA Ops:
  0.6 36.6 %adjoint.1.state = f32[4,384,128]{2,1,0:T(8,128)S(1)} custom-call(f32[384,128]{1,0:T(8,128)} %bitcast.13, f32[384,128]{1,0:T(8,128)} %bitcast.14, f32[384,128]{1,0:T(8,128)} %bitcast.15, f32[384,128]{1,0:T(8,128)} %bitcast.16, f32[384,128]{1,0:T(8,128)} %bitcast.17, f32[384,128]{1,0:T(8,128)} %bitcast.18, s32[2,384,128]{2,1,0:T(8,128)} %bitcast.12, ...), custom_call_target="tpu_custom_call" | custom-call | tf_op jit(solution)/shard_map/adjoint/pallas_call | solution.py:566
  37.3 0.9 %store.1 = (f32[384,128]{1,0:T(8,128)}, f32[384,128]{1,0:T(8,128)}, f32[384,128]{1,0:T(8,128)}, f32[384,128]{1,0:T(8,128)}) custom-call(f32[4,384,128]{2,1,0:T(8,128)S(1)} %adjoint.1.state), custom_call_target="tpu_custom_call" | custom-call | tf_op jit(solution)/shard_map/store/pallas_call | solution.py:577
